TPU v7x, 512 devices: a whole 4x8x8 slice. The times are simulated.
512 devices in a mesh: oy: 8 (over z), ox: 8 (over y_hi, core), ori: 8 (over y_lo, x).
Axes of the slice: x: 4, y: 8 (y_hi: 4, y_lo: 2; y = y_hi * 2 + y_lo), z: 8, core: 2. Of those that a mesh axis runs over, the one named last changes fastest.
Arguments:
- micrograph: float32 [2048, 2048], P('oy', 'ox'), may hold values from -150 to 151
- projections: bfloat16 [64, 192, 192], P(('ox', 'ori')), may hold values from -0.0036315918 to 0.0067443848
- orientations: int32 [16], P('ori'), may hold values from 0 to 63
Outputs:
- best_score: float32 [2048, 2048], P(('oy', 'ori'), 'ox')
- mean_score: float32 [2048, 2048], P(('oy', 'ori'), 'ox')
- mean_square: float32 [2048, 2048], P(('oy', 'ori'), 'ox')
All inputs are finite; a program needn't handle non-finite values.
Results may differ from a plain program's by a relative error of at most 0.0003.
Values may be sent and summed in bfloat16 or wider, within the bound.
A program may use at most 64 MiB of HBM per device.

v0:
```python
import math

import jax
import jax.numpy as jnp
from jax import lax
from jax.sharding import PartitionSpec as P


def with_halo(block, sides, width):
    for axis, dim in sides:
        count = lax.axis_size(axis)
        forward = [(i, i + 1) for i in range(count - 1)]
        backward = [(target, source) for source, target in forward]
        low = lax.ppermute(
            lax.slice_in_dim(block, block.shape[dim] - width, None, axis=dim), axis, forward
        )
        high = lax.ppermute(lax.slice_in_dim(block, 0, width, axis=dim), axis, backward)
        block = jnp.concatenate([low, block, high], axis=dim)
    return block


def combined_all(shard, axis, combine):
    everything = jax.tree.map(lambda part: lax.all_gather(part, axis), shard)
    first = jax.tree.map(lambda part: part[0], everything)

    def turn(k, so_far):
        return combine(so_far, jax.tree.map(lambda part: part[k], everything))

    return lax.fori_loop(1, lax.axis_size(axis), turn, first)


def product(left_op, right_op, accuracy=lax.Precision.HIGHEST):
    return jnp.dot(left_op, right_op, precision=accuracy, preferred_element_type=jnp.float32)


def quick_product(left_op, right_op):
    return product(left_op, right_op, lax.Precision.HIGH)


def twiddles(length):
    row_ids = jnp.arange(length, dtype=jnp.int32)[:, None]
    col_ids = jnp.arange(length, dtype=jnp.int32)[None, :]
    phases = (row_ids * col_ids % length).astype(jnp.float32) * (2.0 * math.pi / length)
    return (jnp.cos(phases), jnp.sin(phases))


def spectrum(extended, cosine, sines):
    inner_re = product(extended, cosine)
    inner_im = -product(extended, sines)
    image_re = product(cosine, inner_re) + product(sines, inner_im)
    image_im = product(cosine, inner_im) - product(sines, inner_re)
    return (image_re, image_im)


def correlate(template, image_re, image_im, cosine, sines, tile_size):
    box_size = template.shape[0]
    length = cosine.shape[0]
    values = template.astype(jnp.float32)
    left_cos = cosine[:, :box_size]
    left_sin = sines[:, :box_size]
    inner_re = quick_product(values, cosine[:box_size, :])
    inner_im = -quick_product(values, sines[:box_size, :])
    templ_re = quick_product(left_cos, inner_re) + quick_product(left_sin, inner_im)
    templ_im = quick_product(left_cos, inner_im) - quick_product(left_sin, inner_re)
    joint_re = image_re * templ_re + image_im * templ_im
    joint_im = image_im * templ_re - image_re * templ_im
    back_cos = cosine[:tile_size, :]
    back_sin = sines[:tile_size, :]
    rows_re = quick_product(back_cos, joint_re) - quick_product(back_sin, joint_im)
    rows_im = quick_product(back_cos, joint_im) + quick_product(back_sin, joint_re)
    result = quick_product(rows_re, cosine[:, :tile_size]) - quick_product(
        rows_im, sines[:, :tile_size]
    )
    return result / float(length * length)


def body(micrograph, projections, orientations):
    tile_size = micrograph.shape[0]
    box_size = projections.shape[1]
    cell_count = float(
        micrograph.shape[0] * micrograph.shape[1] * lax.axis_size("oy") * lax.axis_size("ox")
    )
    image_mean = lax.psum(jnp.sum(micrograph), ("oy", "ox")) / cell_count
    centered = micrograph - image_mean
    variance = lax.psum(jnp.sum(centered * centered), ("oy", "ox")) / cell_count
    normed = centered / jnp.sqrt(variance + 1e-06)
    extended = with_halo(normed, (("oy", 0), ("ox", 1)), box_size // 2)
    cosine, sines = twiddles(extended.shape[0])
    image_re, image_im = spectrum(extended, cosine, sines)
    groups = lax.axis_size("ori")
    my_group = lax.axis_index("ori")
    block_rows = lax.all_gather(projections, ("ox", "ori"), axis=0, tiled=True)
    number = block_rows.shape[0]
    entry_ids = jnp.arange(number, dtype=jnp.int32)
    picker = (orientations[:, None] == entry_ids[None, :]).astype(jnp.bfloat16)
    chosen = jnp.dot(
        picker, block_rows.reshape(number, box_size * box_size), preferred_element_type=jnp.float32
    )
    picked = chosen.astype(jnp.bfloat16)
    templates = picked.reshape(orientations.shape[0], box_size, box_size)
    weights = jnp.ones((orientations.shape[0],), jnp.float32)

    def accumulate(running, element):
        template, weight = element
        correlation = correlate(template, image_re, image_im, cosine, sines, tile_size)
        highest, summed, squared = running
        highest = jnp.maximum(highest, jnp.where(weight > 0, correlation, -jnp.inf))
        return (
            (highest, summed + weight * correlation, squared + weight * correlation * correlation),
            None,
        )

    initial = (
        jnp.full((tile_size, tile_size), -jnp.inf, jnp.float32),
        jnp.zeros((tile_size, tile_size), jnp.float32),
        jnp.zeros((tile_size, tile_size), jnp.float32),
    )
    (highest, summed, squared), _ = lax.scan(accumulate, initial, (templates, weights))
    searched = float(orientations.shape[0] * groups)
    band_rows = tile_size // groups

    def combine(left_stats, right_stats):
        return (
            jnp.maximum(left_stats[0], right_stats[0]),
            left_stats[1] + right_stats[1],
            left_stats[2] + right_stats[2],
        )

    merged = combined_all((highest, summed, squared), "ori", combine)
    offset = my_group * band_rows
    highest = lax.dynamic_slice_in_dim(merged[0], offset, band_rows, 0)
    summed = lax.dynamic_slice_in_dim(merged[1], offset, band_rows, 0)
    squared = lax.dynamic_slice_in_dim(merged[2], offset, band_rows, 0)
    return (highest, summed / searched, squared / searched)


def solution(mesh):
    in_specs = (P("oy", "ox"), P(("ox", "ori"), None, None), P("ori"))
    out_specs = (P(("oy", "ori"), "ox"), P(("oy", "ori"), "ox"), P(("oy", "ori"), "ox"))
    return jax.shard_map(body, mesh=mesh, in_specs=in_specs, out_specs=out_specs, check_vma=False)
```

profile of v0, /device:TPU:16, one launch (start us, length us, event | category | flops | bytes accessed | tf_op | source)
XLA Modules:
  0.0 566.5 jit_solution(18396029633192547639)
XLA Ops:
  7.9 1.6 reduce_sum.18
  9.6 145.4 %psum.14 = f32[]{:T(128)} all-reduce(f32[]{:T(128)} %reduce_sum.18), channel_id=1, replica_groups=mesh['oy'=8,'ox'=8,'ori'=8] {'oy','ox'}, use_global_device_ids=true, to_apply=%region_1.0 | all-reduce | flops 1 | bytes 8 | tf_op jit(solution)/shard_map/psum | solution.py:83
  155.6 1.6 multiply_reduce_fusion
  157.2 139.1 %psum.15 = f32[]{:T(128)} all-reduce(f32[]{:T(128)} %multiply_reduce_fusion), channel_id=1, replica_groups=mesh['oy'=8,'ox'=8,'ori'=8] {'oy','ox'}, use_global_device_ids=true, to_apply=%region_3.0 | all-reduce | flops 1 | bytes 8 | tf_op jit(solution)/shard_map/psum | solution.py:85
  301.8 4.1 collective-permute-done.1
  306.1 1.9 collective-permute-start.2
  308.0 7.1 %collective-permute-start.3 = (f32[448,96]{1,0:T(8,128)S(1)}, f32[448,96]{1,0:T(8,128)}, u32[]{:S(2)}, u32[]{:S(2)}) collective-permute-start(f32[448,96]{1,0:T(8,128)S(1)} %get-tuple-element.453), channel_id=1, source_target_pairs={{8,0},{16,8},{24,16},{32,24},{40,32},{48,40},{56,48},{9,1},{17,9},... | collective-permute-start | bytes 516104 | tf_op jit(solution)/shard_map/ppermute | solution.py:17
  315.1 3.8 fusion.31
  318.9 2.2 collective-permute-done.3
  321.1 6.3 %convolution_negate_fusion.1 = f32[448,448]{1,0:T(8,128)S(1)} fusion(f32[448,96]{1,0:T(8,128)} %collective-permute-done.3, f32[96,256]{1,0:T(8,128)S(1)} %collective-permute-done.1, f32[256,256]{1,0:T(8,128)S(1)} %subtract_divide_fusion, f32[96,256]{1,0:T(8,128)S(1)} %collective-permute-done, f32[448,96]{1,0:T(8,128)} %collective-permute-done.2), kind=kOutput, calls=%fused_computation.45 | convolution fusion | flops 1081794560 | bytes 1605632 | tf_op jit(solution)/shard_map/dot_general | solution.py:33
  327.4 6.8 %fusion.38 = f32[448,448]{1,0:T(8,128)S(1)} fusion(f32[448,96]{1,0:T(8,128)} %collective-permute-done.3, f32[96,256]{1,0:T(8,128)S(1)} %collective-permute-done.1, f32[256,256]{1,0:T(8,128)S(1)} %subtract_divide_fusion, f32[96,256]{1,0:T(8,128)S(1)} %collective-permute-done, f32[448,96]{1,0:T(8,128)} %collective-permute-done.2), kind=kOutput, calls=%fused_computation.58 | convolution fusion | flops 1081593856 | bytes 1605632 | tf_op jit(solution)/shard_map/dot_general | solution.py:33
  334.3 5.2 fusion.34
  339.5 6.9 %convolution_subtract_fusion.3 = f32[448,448]{1,0:T(8,128)} fusion(f32[448,448]{1,0:T(8,128)S(1)} %fusion.34, f32[448,448]{1,0:T(8,128)S(1)} %fusion.38), kind=kOutput, calls=%fused_computation.43 | convolution fusion | flops 1080991744 | bytes 2408448 | tf_op jit(solution)/shard_map/dot_general | solution.py:33
  347.9 6.5 %fusion.36 = f32[448,448]{1,0:T(8,128)S(1)} fusion(f32[448,448]{1,0:T(8,128)} %copy-done.7), kind=kOutput, calls=%fused_computation.57 | convolution fusion | flops 1080791040 | bytes 1605632 | tf_op jit(solution)/shard_map/dot_general | solution.py:33
  354.3 6.4 %convolution_add_fusion.2 = f32[448,448]{1,0:T(8,128)} fusion(f32[448,448]{1,0:T(8,128)S(1)} %fusion.36, f32[448,448]{1,0:T(8,128)S(1)} %copy-done.6), kind=kOutput, calls=%fused_computation.44 | convolution fusion | flops 1080991744 | bytes 2408448 | tf_op jit(solution)/shard_map/dot_general | solution.py:33
  360.7 2.4 copy.8
  363.1 11.1 %reshape.13 = bf16[64,36864]{1,0:T(8,128)(2,1)} reshape(bf16[64,192,192]{2,1,0:T(8,128)(2,1)} %all-gather.8.cloned.1.call-done) | data formatting | bytes 9437184 | tf_op jit(solution)/shard_map/reshape | solution.py:97
  374.2 3.8 convolution_convert_fusion
  378.0 1.8 reshape.14
  379.8 20.0 %while.38 = (s32[]{:T(128)}, f32[256,256]{1,0:T(8,128)S(1)}, f32[256,256]{1,0:T(8,128)S(1)}, f32[256,256]{1,0:T(8,128)S(1)}, bf16[2,192,192]{2,1,0:T(8,128)(2,1)...) while((s32[]{:T(128)}, f32[256,256]{1,0:T(8,128)S(1)}, ...), condition=%wide.region_5.6_spmd.clone.clone, body=%wide.region_4.5_spmd.clone.clone.sunk | while | flops 2710982656 | bytes 29343904 | solution.py:118
  401.9 43.0 %all-gather.12.cloned.1.call-done = f32[2048,256]{1,0:T(8,128)} async-done(((f32[256,256]{1,0:T(8,128)}), f32[2048,256]{1,0:T(8,128)}) %all-gather.12.cloned.1.call-update) | async-done | bytes 2097168 | tf_op jit(solution)/shard_map/all_gather | solution.py:23
  445.8 47.3 %all-gather.10.cloned.1.call-done = f32[2048,256]{1,0:T(8,128)} async-done(((f32[256,256]{1,0:T(8,128)}), f32[2048,256]{1,0:T(8,128)}) %all-gather.10.cloned.1.call-update) | async-done | bytes 2097168 | tf_op jit(solution)/shard_map/all_gather | solution.py:23
  494.1 47.2 %all-gather.14.cloned.1.call-done = f32[2048,256]{1,0:T(8,128)} async-done(((f32[256,256]{1,0:T(8,128)}), f32[2048,256]{1,0:T(8,128)}) %all-gather.14.cloned.1.call-update) | async-done | bytes 2097168 | tf_op jit(solution)/shard_map/all_gather | solution.py:23
  542.2 15.5 %while.37 = (s32[]{:T(128)}, f32[256,256]{1,0:T(8,128)S(1)}, f32[256,256]{1,0:T(8,128)S(1)}, f32[256,256]{1,0:T(8,128)S(1)}, f32[8,256,256]{2,1,0:T(8,128)}, /*i...) while((s32[]{:T(128)}, f32[256,256]{1,0:T(8,128)S(1)}, ...), condition=%wide.region_7.8_spmd, body=%wide.region_6.7_spmd.sunk | while | flops 196613 | bytes 2359439 | solution.py:29
  (83 shorter events, 48.9 us)
Async XLA Ops:
  7.2 356.0 %all-gather.8.cloned.1.call-start = ((), (), s32[]{:S(2)}) async-start(), calls=%async_computation | async-start | bytes 6389760 | tf_op jit(solution)/shard_map/all_gather | solution.py:92
  7.9 436.9 %all-gather.12.cloned.1.call-start = ((), (), s32[]{:S(2)}) async-start(), calls=%async_computation.2 | async-start | bytes 2359296 | tf_op jit(solution)/shard_map/all_gather | solution.py:23
  298.1 3.7 collective-permute-start
  299.4 6.5 %collective-permute-start.1 = (f32[96,256]{1,0:T(8,128)S(1)}, f32[96,256]{1,0:T(8,128)S(1)}, u32[]{:S(2)}, u32[]{:S(2)}) collective-permute-start(f32[96,256]{1,0:T(8,128)S(1)} %get-tuple-element.455), channel_id=1, source_target_pairs={{64,0},{128,64},{192,128},{256,192},{320,256},{384,320},{448,384},... | collective-permute-start | bytes 294920 | tf_op jit(solution)/shard_map/ppermute | solution.py:17
  306.1 12.9 %collective-permute-start.2 = (f32[448,96]{1,0:T(8,128)S(1)}, f32[448,96]{1,0:T(8,128)}, u32[]{:S(2)}, u32[]{:S(2)}) collective-permute-start(f32[448,96]{1,0:T(8,128)S(1)} %get-tuple-element.452), channel_id=1, source_target_pairs={{0,8},{8,16},{16,24},{24,32},{32,40},{40,48},{48,56},{1,9},{9,17},... | collective-permute-start | bytes 516104 | tf_op jit(solution)/shard_map/ppermute | solution.py:14
  308.0 13.1 %collective-permute-start.3 = (f32[448,96]{1,0:T(8,128)S(1)}, f32[448,96]{1,0:T(8,128)}, u32[]{:S(2)}, u32[]{:S(2)}) collective-permute-start(f32[448,96]{1,0:T(8,128)S(1)} %get-tuple-element.453), channel_id=1, source_target_pairs={{8,0},{16,8},{24,16},{32,24},{40,32},{48,40},{56,48},{9,1},{17,9},... | collective-permute-start | bytes 516104 | tf_op jit(solution)/shard_map/ppermute | solution.py:17
  327.4 6.8 %copy-start.5 = (f32[448,448]{1,0:T(8,128)}, f32[448,448]{1,0:T(8,128)S(1)}, u32[]{:S(2)}) copy-start(f32[448,448]{1,0:T(8,128)S(1)} %convolution_negate_fusion.1) | copy-start | bytes 2408452
  334.3 5.2 copy-start.7
  347.9 6.5 %copy-start.6 = (f32[448,448]{1,0:T(8,128)S(1)}, f32[448,448]{1,0:T(8,128)}, u32[]{:S(2)}) copy-start(f32[448,448]{1,0:T(8,128)} %copy-done.5) | copy-start | bytes 2408452
  363.1 11.1 %copy-start.4 = (s32[2]{0:T(128)S(1)}, s32[2]{0:T(128)}, u32[]{:S(2)}) copy-start(s32[2]{0:T(128)} %param.9) | copy-start | bytes 28
  383.1 1.9 copy-start
  393.1 1.9 copy-start
  399.8 0.7 copy-start.2
  399.8 0.8 copy-start.3
  399.8 1.5 copy-start.1
  400.5 92.6 %all-gather.10.cloned.1.call-start = ((), (), s32[]{:S(2)}) async-start(), calls=%async_computation.1 | async-start | bytes 2359296 | tf_op jit(solution)/shard_map/all_gather | solution.py:23
  401.3 140.0 %all-gather.14.cloned.1.call-start = ((), (), s32[]{:S(2)}) async-start(), calls=%async_computation.3 | async-start | bytes 2359296 | tf_op jit(solution)/shard_map/all_gather | solution.py:23
Sparse Core Ops, SparseCore 0:
  10.1 202.7 all-gather.7
  400.7 44.1 all-gather.11
  446.9 46.1 all-gather.9
  495.0 46.1 all-gather.13
where the time goes:
time: 577 us; the launch traced here: 567 us
  blocking collectives  285 us (49%)
  waiting for transfers between devices  147 us (25%)
  matrix products  61.5 us (11%)
  other arithmetic  24.6 us (4%)
  local copies, waits for them, and re-layouts  21.2 us (4%)
  between operations  15.8 us (3%)
  starting transfers between devices  11.8 us (2%)
    psum x1, blocking collectives, body(): image_mean = lax.psum(jnp.sum(micrograph), ('oy', 'ox')) / cell_count  145 us
    psum x1, blocking collectives, body(): variance = lax.psum(jnp.sum(centered * centered), ('oy', 'ox')) / cell_count  139 us
    all_gather x3, waiting for transfers between devices, combined_all(): everything = jax.tree.map(lambda part: lax.all_gather(part, axis), shard)  137 us
    dot_general x30, matrix products, product(): jnp.dot(left_op, right_op, precision=accuracy, preferred_element_type=jnp...  57.7 us
  transfers between devices with their start and end apart: 8, of which 6 were waited for; matrix products, arithmetic and copies ran while one was open for 9% of the time, Pallas kernels for 0%

commit v1 on v0

v1 whole, which is shorter than its diff:
```python
import functools
import math

import jax
import jax.numpy as jnp
import ml_dtypes
import numpy as np
from jax import lax
from jax.experimental import pallas as pl
from jax.experimental.pallas import tpu as pltpu
from jax.sharding import PartitionSpec as P

MESH = pl.DeviceIdType.MESH
BF16 = jnp.bfloat16
F32 = jnp.float32

TILE = 256
BOX = 192
HALF = 96
LEN = 448
FOLD = LEN // 2
PART = 48
BAND = 32
FREQS = LEN // 2 + 1


def trig(rows, cols):
    turns = np.outer(rows, cols) % LEN
    phase = turns * (2.0 * math.pi / LEN)
    return np.cos(phase), np.sin(phase)


def hi_lo(table):
    table = table.astype(np.float32)
    high = table.astype(ml_dtypes.bfloat16)
    low = (table - high.astype(np.float32)).astype(ml_dtypes.bfloat16)
    return np.stack([high, low])


def tables():
    freq = np.arange(256)
    live = freq < FREQS

    def by_tile(re_part, im_part, axis):
        re_lo, re_hi = np.split(re_part, 2, axis)
        im_lo, im_hi = np.split(im_part, 2, axis)
        return np.concatenate([re_lo, im_lo, re_hi, im_hi], axis)

    lane = np.arange(512)
    place = np.where(lane < 352, lane, lane - 64)
    used = (lane < 352) | (lane >= 416)
    cosine, sine = trig(place, freq)
    keep = used[:, None] & live[None, :]
    image_x = by_tile(cosine * keep, -sine * keep, 1)

    near = np.arange(FOLD)
    image_y = np.stack(
        [np.concatenate(trig(2 * near + odd, near), 0) for odd in (0, 1)]
    )

    column = np.arange(256)
    cosine, sine = trig(column - HALF, freq)
    keep = (column < BOX)[:, None] & live[None, :]
    box_x = by_tile(cosine * keep, -sine * keep, 1)

    order = np.concatenate([2 * near, 2 * near + 1])
    box_y = np.concatenate(trig(order, np.arange(BOX) - HALF), 0)

    pixel = np.arange(TILE)
    back_y = np.concatenate(trig(pixel, order), 0)

    cosine, sine = trig(freq, pixel)
    share = np.where((freq == 0) | (freq == FREQS - 1), 1.0, 2.0) * live / (LEN * LEN)
    back_x = by_tile(cosine * share[:, None], -sine * share[:, None], 0)
    return [hi_lo(t) for t in (image_x, image_y, box_x, box_y, back_y, back_x)]


def split(values):
    high = values.astype(BF16)
    return high, (values - high.astype(F32)).astype(BF16)


def mul(left, right):
    return jnp.dot(left, right, preferred_element_type=F32)


def triple(left_hi, left_lo, right_hi, right_lo):
    return mul(left_hi, right_hi) + (mul(left_hi, right_lo) + mul(left_lo, right_hi))


def kernel(
    x_ref, t_ref, o_ref, ix_h, iy_h, bx_h, by_h, ky_h, kx_h,
    best_ref, mean_ref, square_ref,
    ext, ext_hi, ext_lo, own, bank, mine, some, piece, boxes,
    stat_a, stats_a, stat_b, stats_b, image, corr, got,
    ix, iy, bx, by, ky, kx,
    table_sem, halo_s, halo_r, bank_s, bank_r, some_s, some_r, box_s, box_r, pair_s, pair_r,
    sa_s, sa_r, sb_s, sb_r, out_s, out_r,
):
    z = lax.axis_index("oy")
    a = lax.axis_index("ox")
    j = lax.axis_index("ori")
    core = lax.rem(a, 2)
    chip = a // 2
    partner = a + 1 - 2 * core

    def up(v, d):
        return lax.rem(v + d, 8)

    ori_peers = [{"ori": up(j, d)} for d in range(1, 8)]
    pair_peers = [{"ox": partner, "ori": up(j, d)} for d in range(8)]
    oy_peers = [{"oy": up(z, d)} for d in range(1, 8)]
    ox_peers = [{"ox": up(a, d)} for d in range(1, 8)]
    hi_peers = [{"ox": up(a, 2 * d)} for d in range(1, 4)]
    corner_peers = [{"oy": up(z, dz), "ox": up(a, da)} for dz in (1, 7) for da in (1, 7)]

    barrier = pltpu.get_barrier_semaphore()
    greeted = corner_peers + oy_peers + ox_peers + pair_peers[1:] + ori_peers
    for peer in greeted:
        pl.semaphore_signal(barrier, inc=1, device_id=peer, device_id_type=MESH)

    loads = [
        pltpu.make_async_copy(src, dst, table_sem.at[k])
        for k, (src, dst) in enumerate(
            ((ix_h, ix), (iy_h, iy), (bx_h, bx), (by_h, by), (ky_h, ky), (kx_h, kx))
        )
    ]
    for load in loads:
        load.start()

    own[0] = t_ref[0, :, 0:128]
    own[1] = jnp.zeros((BOX, 128), BF16)
    own[1, :, 0 : BOX - 128] = t_ref[0, :, 128:BOX]

    pixels = x_ref[...]
    count = float(TILE * TILE)
    tile_mean = jnp.sum(jnp.sum(pixels, 0, keepdims=True), 1, keepdims=True) / count
    off = pixels - tile_mean
    tile_dev = jnp.sum(jnp.sum(off * off, 0, keepdims=True), 1, keepdims=True)
    row = lax.broadcasted_iota(jnp.int32, (8, 128), 0)
    stat_a[...] = jnp.where(row == 0, tile_mean, tile_dev)

    pl.semaphore_wait(barrier, len(greeted))

    def send(src, dst, s, r, peer):
        copy = pltpu.make_async_remote_copy(
            src_ref=src, dst_ref=dst, send_sem=s, recv_sem=r, device_id=peer, device_id_type=MESH
        )
        copy.start()
        return copy

    strip = lax.rem(z, 4)
    lanes = z // 4
    strip_rows = pl.ds(pl.multiple_of(strip * PART, 16), PART)
    bank_copies = [
        send(own.at[lanes, strip_rows], bank.at[k], bank_s.at[k], bank_r.at[k], peer)
        for k, peer in enumerate(ori_peers + pair_peers)
    ]
    stat_a_copies = [
        send(stat_a, stats_a.at[k], sa_s.at[k], sa_r.at[k], peer) for k, peer in enumerate(oy_peers)
    ]
    row_kind = {0: (0, 256, 0), 7: (0, HALF, 256), 1: (TILE - HALF, HALF, 352)}
    col_kind = {0: (0, 256, 0), 7: (0, 128, 256), 1: (128, 128, 384)}
    halo_copies = []
    for dz in (0, 1, 7):
        for da in (0, 1, 7):
            if dz == 0 and da == 0:
                continue
            r_from, r_size, r_to = row_kind[dz]
            c_from, c_size, c_to = col_kind[da]
            k = len(halo_copies)
            halo_copies.append(
                send(
                    x_ref.at[pl.ds(r_from, r_size), pl.ds(c_from, c_size)],
                    ext.at[pl.ds(r_to, r_size), pl.ds(c_to, c_size)],
                    halo_s.at[k], halo_r.at[k], {"oy": up(z, dz), "ox": up(a, da)},
                )
            )

    want = o_ref[core]
    local = own[lanes, strip_rows, :].astype(F32)
    total = jnp.where(a * 8 + j == want, 1.0, 0.0) * local
    for k, copy in enumerate(bank_copies):
        copy.wait()
        d = k + 1 if k < 7 else k - 7
        column = a if k < 7 else partner
        entry = column * 8 + lax.rem(j + 8 - d, 8)
        total += jnp.where(entry == want, 1.0, 0.0) * bank[k].astype(F32)
    mine[...] = total.astype(BF16)
    some_copies = [
        send(mine, some.at[k], some_s.at[k], some_r.at[k], peer) for k, peer in enumerate(hi_peers)
    ]

    def merge(first, others, number):
        means = [first[0:1, :]] + [others[k, 0:1, :] for k in range(7)]
        devs = [first[1:2, :]] + [others[k, 1:2, :] for k in range(7)]
        mid = sum(means) * 0.125
        dev = sum(devs) + number * sum((m - mid) * (m - mid) for m in means)
        return mid, dev

    for copy in stat_a_copies:
        copy.wait()
    mid, dev = merge(stat_a, stats_a, count)
    stat_b[...] = jnp.where(row == 0, mid, dev)
    stat_b_copies = [
        send(stat_b, stats_b.at[k], sb_s.at[k], sb_r.at[k], peer) for k, peer in enumerate(ox_peers)
    ]

    total = mine[...].astype(F32)
    for k, copy in enumerate(some_copies):
        copy.wait()
        total += some[k].astype(F32)
    piece[...] = total.astype(BF16)
    box_copies = [
        send(piece, boxes.at[0, lanes, strip_rows], box_s.at[k], box_r.at[k], peer)
        for k, peer in enumerate(oy_peers)
    ]
    boxes[0, lanes, strip_rows, :] = piece[...]

    for copy in stat_b_copies:
        copy.wait()
    mid, dev = merge(stat_b, stats_b, count * 8)
    scale = 1.0 / jnp.sqrt(dev / (count * 64) + 1e-06)
    mid, scale = mid[:, 0:1], scale[:, 0:1]
    for copy in halo_copies:
        copy.wait()
    for r_at, r_size, r_ok in ((0, 256, None), (256, HALF, z < 7), (352, HALF, z > 0)):
        for c_at, c_size, c_ok in ((0, 256, None), (256, 128, a < 7), (384, 128, a > 0)):
            inside = scale
            for ok in (r_ok, c_ok):
                if ok is not None:
                    inside = inside * jnp.where(ok, 1.0, 0.0)
            if r_at == 0 and c_at == 0:
                values = pixels
            else:
                values = ext[r_at : r_at + r_size, c_at : c_at + c_size]
            high, low = split((values - mid) * inside)
            ext_hi[r_at : r_at + r_size, c_at : c_at + c_size] = high
            ext_lo[r_at : r_at + r_size, c_at : c_at + c_size] = low

    for load in loads:
        load.wait()

    def rotate(both, size):
        low, high = both[:size], both[size:]
        return jnp.concatenate(
            [low[:, :128] + high[:, 128:], low[:, 128:] - high[:, :128]], axis=1
        )

    def image_tile(tau, _):
        at = pl.ds(pl.multiple_of(tau * 256, 256), 256)
        lines = triple(ext_hi[...], ext_lo[...], ix[0, :, at], ix[1, :, at])
        upper, lower = lines[:FOLD], lines[FOLD:]
        for odd, folded in ((0, upper + lower), (1, upper - lower)):
            high, low = split(folded)
            both = triple(iy[0, odd], iy[1, odd], high, low)
            image[pl.ds(odd * FOLD, FOLD), at] = rotate(both, FOLD)
        return _

    lax.fori_loop(0, 2, image_tile, 0)

    for copy in box_copies:
        copy.wait()
    pair_copy = send(boxes.at[0], boxes.at[1], pair_s, pair_r, {"ox": partner})

    out_copies = []
    for slot in range(2):
        if slot == 1:
            pair_copy.wait()
        box = jnp.concatenate([boxes[slot, 0], boxes[slot, 1]], axis=1)

        def slot_tile(tau, _, box=box, slot=slot):
            at = pl.ds(pl.multiple_of(tau * 256, 256), 256)
            high, low = split(mul(box, bx[0, :, at]) + mul(box, bx[1, :, at]))
            wave = rotate(triple(by[0], by[1], high, low), LEN)
            t_re, t_im = wave[:, :128], wave[:, 128:]
            g = image[:, at]
            g_re, g_im = g[:, :128], g[:, 128:]
            joint = jnp.concatenate(
                [g_re * t_re + g_im * t_im, g_im * t_re - g_re * t_im], axis=1
            )
            high, low = split(joint)
            both = triple(ky[0], ky[1], high, low)
            low_half, high_half = both[:TILE], both[TILE:]
            lines = jnp.concatenate(
                [low_half[:, :128] - high_half[:, 128:], low_half[:, 128:] + high_half[:, :128]],
                axis=1,
            )
            high, low = split(lines)
            part = triple(high, low, kx[0, at, :], kx[1, at, :])

            if True:
                corr[slot] = jnp.where(tau == 0, part, corr[slot] + part)
            return _

        corr[slot] = jnp.zeros((TILE, TILE), F32)
        lax.fori_loop(0, 2, slot_tile, 0)
        for d in range(1, 8):
            to = lax.rem(j + d, 8)
            k = slot * 7 + d - 1
            out_copies.append(
                send(
                    corr.at[slot, pl.ds(pl.multiple_of(to * BAND, BAND), BAND)],
                    got.at[k], out_s.at[k], out_r.at[k], {"ori": to},
                )
            )

    band = pl.ds(pl.multiple_of(j * BAND, BAND), BAND)
    one, two = corr[0, band, :], corr[1, band, :]
    best = jnp.maximum(one, two)
    summed = one + two
    squared = one * one + two * two
    for k, copy in enumerate(out_copies):
        copy.wait()
        value = got[k]
        best = jnp.maximum(best, value)
        summed += value
        squared += value * value
    best_ref[...] = best
    mean_ref[...] = summed / 16.0
    square_ref[...] = squared / 16.0


def body(micrograph, projections, orientations):
    consts = tables()
    vmem = pl.BlockSpec(memory_space=pltpu.VMEM)
    hbm = pl.BlockSpec(memory_space=pl.ANY)
    dma = pltpu.SemaphoreType.DMA
    out = jax.ShapeDtypeStruct((BAND, TILE), F32)
    scratch = [
        pltpu.VMEM((LEN, 512), F32),
        pltpu.VMEM((LEN, 512), BF16),
        pltpu.VMEM((LEN, 512), BF16),
        pltpu.VMEM((2, BOX, 128), BF16),
        pltpu.VMEM((15, PART, 128), BF16),
        pltpu.VMEM((PART, 128), BF16),
        pltpu.VMEM((3, PART, 128), BF16),
        pltpu.VMEM((PART, 128), BF16),
        pltpu.VMEM((2, 2, BOX, 128), BF16),
        pltpu.VMEM((8, 128), F32),
        pltpu.VMEM((7, 8, 128), F32),
        pltpu.VMEM((8, 128), F32),
        pltpu.VMEM((7, 8, 128), F32),
        pltpu.VMEM((LEN, 512), F32),
        pltpu.VMEM((2, TILE, TILE), F32),
        pltpu.VMEM((14, BAND, TILE), F32),
    ]
    scratch += [pltpu.VMEM(c.shape, BF16) for c in consts]
    scratch += [dma((6,))]
    for n in (8, 15, 3, 7):
        scratch += [dma((n,)), dma((n,))]
    scratch += [dma, dma]
    for n in (7, 7, 14):
        scratch += [dma((n,)), dma((n,))]
    return pl.pallas_call(
        kernel,
        out_shape=(out, out, out),
        in_specs=[vmem, vmem, pl.BlockSpec(memory_space=pltpu.SMEM)] + [hbm] * 6,
        out_specs=(vmem, vmem, vmem),
        scratch_shapes=scratch,
        name="match",
        compiler_params=pltpu.CompilerParams(
            collective_id=0, has_side_effects=True, vmem_limit_bytes=48 * 1024 * 1024
        ),
    )(micrograph, projections, orientations, *[jnp.asarray(c) for c in consts])


def solution(mesh):
    in_specs = (P("oy", "ox"), P(("ox", "ori"), None, None), P("ori"))
    out_specs = (P(("oy", "ori"), "ox"), P(("oy", "ori"), "ox"), P(("oy", "ori"), "ox"))
    return jax.shard_map(body, mesh=mesh, in_specs=in_specs, out_specs=out_specs, check_vma=False)
```

time: 577 us -> 58.6 us (0.10)
  the two profiles are of different devices: /device:TPU:16 before, /device:TPU:1 now
where the time goes in v1:
time: 58.6 us; the launch traced here: 57.9 us
  Pallas kernels  46 us (78%)
  local copies, waits for them, and re-layouts  11.2 us (19%)
  between operations  0.66 us (1%)
    pallas_call x1, Pallas kernels, body(): pl.pallas_call(kernel, out_shape=(out, out, out), in_specs=[vmem, vmem, p...  46 us
    unnamed x21, local copies, waits for them, and re-layouts  11.2 us

profile of v1, /device:TPU:1, one launch (start us, length us, event | category | flops | bytes accessed | tf_op | source)
XLA Modules:
  0.0 57.9 jit_solution(13681545006159248710)
XLA Ops:
  0.6 0.0 copy-start
  0.6 1.2 %copy-done = bf16[2,512,448]{2,1,0:T(8,128)(2,1)S(1)} copy-done((bf16[2,512,448]{2,1,0:T(8,128)(2,1)S(1)}, bf16[2,512,448]{2,1,0:T(8,128)(2,1)}, u32[]{:S(2)}) %copy-start) | copy-done | bytes 917528
  1.9 0.0 copy-start.1
  1.9 1.2 %copy-done.1 = bf16[2,512,512]{2,1,0:T(8,128)(2,1)S(1)} copy-done((bf16[2,512,512]{2,1,0:T(8,128)(2,1)S(1)}, bf16[2,512,512]{2,1,0:T(8,128)(2,1)}, u32[]{:S(2)}) %copy-start.1) | copy-done | bytes 1048600
  3.1 0.0 copy-start.2
  3.1 1.2 %copy-done.2 = bf16[2,896,192]{2,1,0:T(8,128)(2,1)S(1)} copy-done((bf16[2,896,192]{2,1,0:T(8,128)(2,1)S(1)}, bf16[2,896,192]{2,1,0:T(8,128)(2,1)}, u32[]{:S(2)}) %copy-start.2) | copy-done | bytes 688152
  4.3 0.0 copy-start.3
  4.3 1.2 %copy-done.3 = bf16[2,2,448,224]{3,2,1,0:T(8,128)(2,1)S(1)} copy-done((bf16[2,2,448,224]{3,2,1,0:T(8,128)(2,1)S(1)}, bf16[2,2,448,224]{3,2,1,0:T(8,128)(2,1)}, u32[]{:S(2)}) %copy-start.3) | copy-done | bytes 802840
  5.4 0.0 copy-start.4
  5.4 1.0 %copy-done.4 = bf16[2,512,256]{2,1,0:T(8,128)(2,1)S(1)} copy-done((bf16[2,512,256]{2,1,0:T(8,128)(2,1)S(1)}, bf16[2,512,256]{2,1,0:T(8,128)(2,1)}, u32[]{:S(2)}) %copy-start.4) | copy-done | bytes 524312
  6.5 0.0 copy-start.5
  6.5 1.0 %copy-done.5 = bf16[2,256,512]{2,1,0:T(8,128)(2,1)S(1)} copy-done((bf16[2,256,512]{2,1,0:T(8,128)(2,1)S(1)}, bf16[2,256,512]{2,1,0:T(8,128)(2,1)}, u32[]{:S(2)}) %copy-start.5) | copy-done | bytes 524312
  7.5 0.0 copy-start.6
  7.5 0.9 %copy-done.6 = f32[256,256]{1,0:T(8,128)S(1)} copy-done((f32[256,256]{1,0:T(8,128)S(1)}, f32[256,256]{1,0:T(8,128)}, u32[]{:S(2)}) %copy-start.6) | copy-done | bytes 262168
  8.5 0.0 copy-start.7
  8.5 0.9 %copy-done.7 = bf16[1,192,192]{2,1,0:T(8,128)(2,1)S(1)} copy-done((bf16[1,192,192]{2,1,0:T(8,128)(2,1)S(1)}, bf16[1,192,192]{2,1,0:T(8,128)(2,1)}, u32[]{:S(2)}) %copy-start.7) | copy-done | bytes 73752
  9.4 0.0 copy-start.8
  9.4 0.7 %copy-done.8 = s32[2]{0:T(128)S(1)} copy-done((s32[2]{0:T(128)S(1)}, s32[2]{0:T(128)}, u32[]{:S(2)}) %copy-start.8) | copy-done | bytes 32
  10.0 46.0 %match.1 = (f32[32,256]{1,0:T(8,128)S(1)}, f32[32,256]{1,0:T(8,128)S(1)}, f32[32,256]{1,0:T(8,128)S(1)}) custom-call(f32[256,256]{1,0:T(8,128)S(1)} %copy-done.6, bf16[1,192,192]{2,1,0:T(8,128)(2,1)S(1)} %copy-done.7, s32[2]{0:T(128)S(1)} %copy-done.8, bf16[2,512,512]{2,1,0:T(8,128)(2,1)S(1)} %copy-done.1, bf16[2,2,448,224]{3,2,1,0:T(8,128)(2,1)S(1)} %copy-done.3, ...), custom_call_target="tpu_custom_call" | custom-call | tf_op jit(solution)/shard_map/match/pallas_call | solution.py:355
  56.1 0.6 %copy.15 = f32[32,256]{1,0:T(8,128)} copy(f32[32,256]{1,0:T(8,128)S(1)} %get-tuple-element.6) | data formatting | bytes 65536
  56.7 0.6 %copy.16 = f32[32,256]{1,0:T(8,128)} copy(f32[32,256]{1,0:T(8,128)S(1)} %get-tuple-element.7) | data formatting | bytes 65536
  57.3 0.6 %copy.17 = f32[32,256]{1,0:T(8,128)} copy(f32[32,256]{1,0:T(8,128)S(1)} %get-tuple-element.8) | data formatting | bytes 65536
Async XLA Ops:
  0.6 1.2 %copy-start = (bf16[2,512,448]{2,1,0:T(8,128)(2,1)S(1)}, bf16[2,512,448]{2,1,0:T(8,128)(2,1)}, u32[]{:S(2)}) copy-start(bf16[2,512,448]{2,1,0:T(8,128)(2,1)} %constant.16.clone.ky_h) | copy-start | bytes 2752516
  1.9 1.2 %copy-start.1 = (bf16[2,512,512]{2,1,0:T(8,128)(2,1)S(1)}, bf16[2,512,512]{2,1,0:T(8,128)(2,1)}, u32[]{:S(2)}) copy-start(bf16[2,512,512]{2,1,0:T(8,128)(2,1)} %constant.12.clone.ix_h) | copy-start | bytes 3145732
  3.1 1.2 %copy-start.2 = (bf16[2,896,192]{2,1,0:T(8,128)(2,1)S(1)}, bf16[2,896,192]{2,1,0:T(8,128)(2,1)}, u32[]{:S(2)}) copy-start(bf16[2,896,192]{2,1,0:T(8,128)(2,1)} %constant.15.clone.by_h) | copy-start | bytes 2064388
  4.3 1.2 %copy-start.3 = (bf16[2,2,448,224]{3,2,1,0:T(8,128)(2,1)S(1)}, bf16[2,2,448,224]{3,2,1,0:T(8,128)(2,1)}, u32[]{:S(2)}) copy-start(bf16[2,2,448,224]{3,2,1,0:T(8,128)(2,1)} %constant.13.clone.iy_h) | copy-start | bytes 2408452
  5.4 1.0 %copy-start.4 = (bf16[2,512,256]{2,1,0:T(8,128)(2,1)S(1)}, bf16[2,512,256]{2,1,0:T(8,128)(2,1)}, u32[]{:S(2)}) copy-start(bf16[2,512,256]{2,1,0:T(8,128)(2,1)} %constant.17.clone.kx_h) | copy-start | bytes 1572868
  6.5 1.0 %copy-start.5 = (bf16[2,256,512]{2,1,0:T(8,128)(2,1)S(1)}, bf16[2,256,512]{2,1,0:T(8,128)(2,1)}, u32[]{:S(2)}) copy-start(bf16[2,256,512]{2,1,0:T(8,128)(2,1)} %constant.14.clone.bx_h) | copy-start | bytes 1572868
  7.5 0.9 %copy-start.6 = (f32[256,256]{1,0:T(8,128)S(1)}, f32[256,256]{1,0:T(8,128)}, u32[]{:S(2)}) copy-start(f32[256,256]{1,0:T(8,128)} %x_ref.1) | copy-start | bytes 786436
  8.5 0.9 %copy-start.7 = (bf16[1,192,192]{2,1,0:T(8,128)(2,1)S(1)}, bf16[1,192,192]{2,1,0:T(8,128)(2,1)}, u32[]{:S(2)}) copy-start(bf16[1,192,192]{2,1,0:T(8,128)(2,1)} %t_ref.1) | copy-start | bytes 221188
  9.4 0.7 %copy-start.8 = (s32[2]{0:T(128)S(1)}, s32[2]{0:T(128)}, u32[]{:S(2)}) copy-start(s32[2]{0:T(128)} %o_ref.1) | copy-start | bytes 28

commit v2 on v1

v2 whole, which is shorter than its diff:
```python
import functools
import math

import jax
import jax.numpy as jnp
import ml_dtypes
import numpy as np
from jax import lax
from jax.experimental import pallas as pl
from jax.experimental.pallas import tpu as pltpu
from jax.sharding import PartitionSpec as P

MESH = pl.DeviceIdType.MESH
BF16 = jnp.bfloat16
F32 = jnp.float32

TILE = 256
BOX = 192
HALF = 96
LEN = 448
FOLD = LEN // 2
PART = 96
BAND = 32
FREQS = LEN // 2 + 1


def trig(rows, cols):
    turns = np.outer(rows, cols) % LEN
    phase = turns * (2.0 * math.pi / LEN)
    return np.cos(phase), np.sin(phase)


def stacked(table, axis, order):
    table = table.astype(np.float32)
    high = table.astype(ml_dtypes.bfloat16)
    low = (table - high.astype(np.float32)).astype(ml_dtypes.bfloat16)
    return np.concatenate([{"h": high, "l": low}[c] for c in order], axis)


def waves(freqs, places):
    cosine, sine = trig(freqs, places)
    if freqs[0] == 0:
        sine[0] = np.cos(math.pi * places)
    return cosine, sine


def tables():
    freq = np.arange(256)
    live = freq < FREQS

    def by_tile(re_part, im_part, axis):
        re_lo, re_hi = np.split(re_part, 2, axis)
        im_lo, im_hi = np.split(im_part, 2, axis)
        return np.concatenate([re_lo, im_lo, re_hi, im_hi], axis)

    lane = np.arange(512)
    place = np.where(lane < 352, lane, lane - 64)
    used = (lane < 352) | (lane >= 416)
    cosine, sine = trig(place, freq)
    keep = used[:, None] & live[None, :]
    image_x = stacked(by_tile(cosine * keep, -sine * keep, 1), 0, "hhl")

    near = np.arange(FOLD)
    even, odd = np.arange(0, FOLD, 2), np.arange(1, FOLD, 2)
    image_y = stacked(np.stack([np.concatenate(waves(k, near), 0) for k in (even, odd)]), 2, "hhl")

    column = np.arange(256)
    cosine, sine = trig(column - HALF, freq)
    keep = (column < BOX)[:, None] & live[None, :]
    box_x = stacked(by_tile(cosine * keep, -sine * keep, 1), 0, "hl")

    order = np.concatenate([even, odd])
    box_y = stacked(np.concatenate(waves(order, np.arange(BOX) - HALF), 0), 1, "hhl")

    pixel = np.arange(TILE)
    back_y = stacked(np.concatenate([w.T for w in waves(order, pixel)], 1), 1, "hhl")

    cosine, sine = trig(freq, pixel)
    share = np.where((freq == 0) | (freq == FREQS - 1), 1.0, 2.0) * live / (LEN * LEN)
    back_x = by_tile(cosine * share[:, None], -sine * share[:, None], 0)
    back_x = stacked(back_x.reshape(2, 256, TILE), 1, "hhl")
    return [image_x, image_y, box_x, box_y, back_y, back_x]


def split(values):
    high = values.astype(BF16)
    return high, (values - high.astype(F32)).astype(BF16)


def mul(left, right):
    return jnp.dot(left, right, preferred_element_type=F32)


def left_of(values, axis=0):
    high, low = split(values)
    return jnp.concatenate([high, low, high], axis=axis)


def both_ways(both):
    even, odd = both[:FOLD], both[FOLD:]
    first = lax.broadcasted_iota(jnp.int32, even.shape, 0) == 0
    turned = jnp.concatenate([odd[:, 128:], -odd[:, :128]], axis=1)
    plus = even + jnp.where(first, 0.0, turned)
    minus = jnp.where(first, odd, even - turned)
    return plus, minus


def conj_product(g, t):
    g_re, g_im, t_re, t_im = g[:, :128], g[:, 128:], t[:, :128], t[:, 128:]
    return g_re * t_re + g_im * t_im, g_im * t_re - g_re * t_im


def kernel(
    x_ref, t_ref, o_ref, ix_h, iy_h, bx_h, by_h, ky_h, kx_h,
    out_ref,
    pixels_in, box_in, wanted, ext, ext_hi, ext_lo, own, bank, mine, some, piece, boxes,
    stat_a, stats_a, stat_b, stats_b, image, corr, got,
    ix, iy, bx, by, ky, kx,
    own_sem, table_sem, halo_s, halo_r, bank_s, bank_r, some_s, some_r, box_s, box_r,
    down_s, up_s, sa_r, sb_s, sb_r, out_s, out_r,
):
    z = lax.axis_index("oy")
    a = lax.axis_index("ox")
    j = lax.axis_index("ori")
    core = lax.rem(a, 2)
    partner = a + 1 - 2 * core
    half = lax.rem(z, 2)
    beside = z + 1 - 2 * half

    def turn(v, d):
        return lax.rem(v + d, 8)

    ori_peers = [{"ori": turn(j, d)} for d in range(1, 8)]
    pair_peers = [{"ox": partner, "ori": turn(j, d)} for d in range(8)]
    ox_peers = [{"ox": turn(a, d)} for d in range(1, 8)]
    hi_peers = [{"ox": turn(a, 2 * d)} for d in range(1, 4)]
    box_peers = [{"ox": partner}, {"oy": beside}, {"oy": beside, "ox": partner}]

    barrier = pltpu.get_barrier_semaphore()

    def greet(peer):
        pl.semaphore_signal(barrier, inc=1, device_id=peer, device_id_type=MESH)

    sides = ((1, z < 7, z > 0), (-1, z > 0, z < 7))
    for dz, there, _ in sides:

        @pl.when(there)
        def _(dz=dz):
            greet({"oy": z + dz})

    for peer in ox_peers + pair_peers[1:] + ori_peers + box_peers[2:]:
        greet(peer)
    for d in range(2, 8):

        @pl.when(z + d < 8)
        def _(d=d):
            greet({"oy": z + d})

    greetings = (
        22
        + jnp.where(z > 0, 1, 0)
        + jnp.where(z < 7, 1, 0)
        + jnp.where(z > 1, z - 1, 0)
    )

    own_loads = [
        pltpu.make_async_copy(src, dst, own_sem.at[k])
        for k, (src, dst) in enumerate(((x_ref, pixels_in), (t_ref, box_in), (o_ref, wanted)))
    ]
    loads = [
        pltpu.make_async_copy(src, dst, table_sem.at[k])
        for k, (src, dst) in enumerate(
            ((ix_h, ix), (iy_h, iy), (bx_h, bx), (by_h, by), (ky_h, ky), (kx_h, kx))
        )
    ]
    for load in own_loads + loads:
        load.start()
    for load in own_loads:
        load.wait()

    own[0] = box_in[0, :, 0:128]
    own[1] = jnp.zeros((BOX, 128), BF16)
    own[1, :, 0 : BOX - 128] = box_in[0, :, 128:BOX]

    pixels = pixels_in[...]
    count = float(TILE * TILE)
    tile_mean = jnp.sum(jnp.sum(pixels, 0, keepdims=True), 1, keepdims=True) / count
    off = pixels - tile_mean
    tile_dev = jnp.sum(jnp.sum(off * off, 0, keepdims=True), 1, keepdims=True)
    row = lax.broadcasted_iota(jnp.int32, (8, 128), 0)
    stat_a[...] = jnp.where(row == 0, tile_mean, tile_dev)
    stats_a[z] = stat_a[...]

    pl.semaphore_wait(barrier, greetings)

    def copier(src, dst, s, r, peer):
        return pltpu.make_async_remote_copy(
            src_ref=src, dst_ref=dst, send_sem=s, recv_sem=r, device_id=peer, device_id_type=MESH
        )

    def send(*what):
        copy = copier(*what)
        copy.start()
        return copy

    mid_rows = pl.ds(pl.multiple_of(half * PART, 16), PART)
    bank_copies = [
        send(
            own.at[core if k < 7 else 1 - core, mid_rows],
            bank.at[k], bank_s.at[k], bank_r.at[k], peer,
        )
        for k, peer in enumerate(ori_peers + pair_peers)
    ]

    def tell(d, s):
        return copier(stat_a, stats_a.at[z], s.at[abs(d) - 1], sa_r.at[z], {"oy": z + d})

    def heard(d):
        copier(stat_a, stats_a.at[z + d], up_s.at[0], sa_r.at[z + d], {"oy": z + d}).wait_recv()

    for d in range(1, 8):

        @pl.when(z - d >= 0)
        def _(d=d):
            tell(-d, down_s).start()

    row_kind = {-1: (0, 256), 1: (TILE - HALF, 352)}
    across = [
        send(
            pixels_in.at[:, pl.ds(c_from, 128)], ext.at[pl.ds(0, TILE), pl.ds(c_to, 128)],
            halo_s.at[k], halo_r.at[k], {"ox": turn(a, da)},
        )
        for k, (da, c_from, c_to) in enumerate(((1, 128, 384), (7, 0, 256)))
    ]

    def along(k, dz, source, lanes):
        r_from, r_to = row_kind[dz]
        return copier(
            source.at[pl.ds(r_from, HALF), lanes], ext.at[pl.ds(r_to, HALF), lanes],
            halo_s.at[k], halo_r.at[k], {"oy": z + dz},
        )

    def straight(n):
        return along(2 + n, sides[n][0], pixels_in, pl.ds(0, 256))

    def corners(n):
        return along(4 + n, sides[n][0], ext, pl.ds(256, 256))

    for n in range(2):

        @pl.when(sides[n][1])
        def _(n=n):
            straight(n).start()

    totals = []
    for slot in range(2):
        local = own[core, mid_rows, :].astype(F32)
        totals.append(jnp.where(a * 8 + j == wanted[slot], 1.0, 0.0) * local)
    for k, copy in enumerate(bank_copies):
        copy.wait()
        d = k + 1 if k < 7 else k - 7
        column = a if k < 7 else partner
        entry = column * 8 + lax.rem(j + 8 - d, 8)
        arrived = bank[k].astype(F32)
        for slot in range(2):
            totals[slot] += jnp.where(entry == wanted[slot], 1.0, 0.0) * arrived
    some_copies = []
    for slot in range(2):
        mine[slot] = totals[slot].astype(BF16)
        for k, peer in enumerate(hi_peers):
            n = slot * 3 + k
            some_copies.append(send(mine.at[slot], some.at[n], some_s.at[n], some_r.at[n], peer))

    def merge(tiles, number):
        means = [t[0:1, :] for t in tiles]
        mid = sum(means) * 0.125
        dev = sum(t[1:2, :] for t in tiles) + number * sum((m - mid) * (m - mid) for m in means)
        return mid, dev

    for copy in across:
        copy.wait()
    for n in range(2):

        @pl.when(sides[n][1])
        def _(n=n):
            corners(n).start()

    for copy_of in (straight, corners):
        for n in range(2):

            @pl.when(sides[n][1])
            def _(n=n, copy_of=copy_of):
                copy_of(n).wait_send()

            @pl.when(sides[n][2])
            def _(n=n, copy_of=copy_of):
                copy_of(n).wait_recv()

    for r_at, r_size, r_ok in ((0, 256, None), (256, HALF, z < 7), (352, HALF, z > 0)):
        for c_at, c_size, c_ok in ((0, 256, None), (256, 128, a < 7), (384, 128, a > 0)):
            if r_at == 0 and c_at == 0:
                values = pixels_in[...] - tile_mean
            else:
                values = ext[r_at : r_at + r_size, c_at : c_at + c_size] - tile_mean
            for ok in (r_ok, c_ok):
                if ok is not None:
                    values = jnp.where(ok, values, 0.0)
            high, low = split(values)
            ext_hi[r_at : r_at + r_size, c_at : c_at + c_size] = high
            ext_lo[r_at : r_at + r_size, c_at : c_at + c_size] = low

    for load in loads:
        load.wait()

    for tau in range(2):
        at = slice(tau * 256, tau * 256 + 256)
        whole = jnp.concatenate([ext_hi[...], ext_lo[...], ext_hi[...]], axis=1)
        lines = mul(whole, ix[:, at])
        upper, lower = lines[:FOLD], lines[FOLD:]
        even = mul(iy[0], left_of(upper + lower))
        odd = mul(iy[1], left_of(upper - lower))
        quarter = FOLD // 2
        image[0, :, at], image[1, :, at] = both_ways(
            jnp.concatenate([even[:quarter], odd[:quarter], even[quarter:], odd[quarter:]], axis=0)
        )

    for d in range(1, 8):

        @pl.when(z + d < 8)
        def _(d=d):
            heard(d)
            tell(d, up_s).start()

    box_copies = []
    for slot in range(2):
        total = mine[slot].astype(F32)
        for k in range(3):
            some_copies[slot * 3 + k].wait()
            total += some[slot * 3 + k].astype(F32)
        piece[slot] = total.astype(BF16)
        boxes[slot, core, mid_rows, :] = piece[slot]
        for k, peer in enumerate(box_peers):
            n = slot * 3 + k
            box_copies.append(
                send(piece.at[slot], boxes.at[slot, core, mid_rows], box_s.at[n], box_r.at[n], peer)
            )

    for d in range(1, 8):

        @pl.when(z - d >= 0)
        def _(d=d):
            heard(-d)

    mid, dev = merge([stats_a.at[k] for k in range(8)], count)
    stat_b[...] = jnp.where(row == 0, mid, dev)
    stat_copies = [
        send(stat_b, stats_b.at[k], sb_s.at[k], sb_r.at[k], peer) for k, peer in enumerate(ox_peers)
    ]

    y_at = lax.broadcasted_iota(jnp.int32, (TILE, BOX), 0)
    u_at = lax.broadcasted_iota(jnp.int32, (TILE, BOX), 1)
    line = z * TILE + y_at + u_at - HALF
    row_in = jnp.where((line >= 0) & (line < 8 * TILE), 1.0, 0.0).astype(BF16)
    v_at = lax.broadcasted_iota(jnp.int32, (TILE, TILE), 0)
    x_at = lax.broadcasted_iota(jnp.int32, (TILE, TILE), 1)
    line = a * TILE + x_at + v_at - HALF
    col_in = jnp.where((line >= 0) & (line < 8 * TILE), 1.0, 0.0).astype(BF16)

    out_copies = []
    for slot in range(2):
        for k in range(3):
            box_copies[slot * 3 + k].wait()
        box = jnp.concatenate([boxes[slot, 0], boxes[slot, 1]], axis=1)

        twice = jnp.concatenate([box, box], axis=1)
        parts = []
        for tau in range(2):
            at = slice(tau * 256, tau * 256 + 256)
            t_plus, t_minus = both_ways(mul(by[...], left_of(mul(twice, bx[:, at]))))
            p_re, p_im = conj_product(image[0, :, at], t_plus)
            m_re, m_im = conj_product(image[1, :, at], t_minus)
            first = lax.broadcasted_iota(jnp.int32, (FOLD, 128), 0) == 0
            joint = jnp.concatenate(
                [
                    jnp.concatenate(
                        [p_re + jnp.where(first, 0.0, m_re), p_im + jnp.where(first, 0.0, m_im)],
                        axis=1,
                    ),
                    jnp.concatenate(
                        [jnp.where(first, m_re, m_im - p_im), jnp.where(first, m_im, p_re - m_re)],
                        axis=1,
                    ),
                ],
                axis=0,
            )
            parts.append(mul(left_of(mul(ky[...], left_of(joint)), 1), kx[tau]))
        high, low = split(mul(row_in, box))
        cover = mul(high, col_in) + mul(low, col_in)

        if slot == 0:
            for copy in stat_copies:
                copy.wait()
            mid, dev = merge([stat_b] + [stats_b.at[k] for k in range(7)], count * 8)
            scale = 1.0 / jnp.sqrt(dev[:, 0:1] / (count * 64) + 1e-06)
            rest = mid[:, 0:1] - tile_mean
        corr[slot] = parts[0] + parts[1] - rest * cover

        for d in range(1, 8):
            to = turn(j, d)
            k = slot * 7 + d - 1
            out_copies.append(
                send(
                    corr.at[slot, pl.ds(pl.multiple_of(to * BAND, BAND), BAND)],
                    got.at[k], out_s.at[k], out_r.at[k], {"ori": to},
                )
            )

    band = pl.ds(pl.multiple_of(j * BAND, BAND), BAND)
    one, two = corr[0, band, :], corr[1, band, :]
    best = jnp.maximum(one, two)
    summed = one + two
    squared = one * one + two * two
    for k, copy in enumerate(out_copies):
        copy.wait()
        value = got[k]
        best = jnp.maximum(best, value)
        summed += value
        squared += value * value
    out_ref[0] = best * scale
    out_ref[1] = summed * scale
    out_ref[2] = squared * (scale * scale)
    for d in range(1, 8):

        @pl.when(z - d >= 0)
        def _(d=d):
            tell(-d, down_s).wait_send()

        @pl.when(z + d < 8)
        def _(d=d):
            tell(d, up_s).wait_send()


def body(micrograph, projections, orientations):
    consts = tables()
    vmem = pl.BlockSpec(memory_space=pltpu.VMEM)
    hbm = pl.BlockSpec(memory_space=pl.ANY)
    dma = pltpu.SemaphoreType.DMA
    out = jax.ShapeDtypeStruct((3, BAND, TILE), F32)
    scratch = [
        pltpu.VMEM((TILE, TILE), F32),
        pltpu.VMEM((1, BOX, BOX), BF16),
        pltpu.SMEM((2,), jnp.int32),
        pltpu.VMEM((LEN, 512), F32),
        pltpu.VMEM((LEN, 512), BF16),
        pltpu.VMEM((LEN, 512), BF16),
        pltpu.VMEM((2, BOX, 128), BF16),
        pltpu.VMEM((15, PART, 128), BF16),
        pltpu.VMEM((2, PART, 128), BF16),
        pltpu.VMEM((6, PART, 128), BF16),
        pltpu.VMEM((2, PART, 128), BF16),
        pltpu.VMEM((2, 2, BOX, 128), BF16),
        pltpu.VMEM((8, 128), F32),
        pltpu.VMEM((8, 8, 128), F32),
        pltpu.VMEM((8, 128), F32),
        pltpu.VMEM((7, 8, 128), F32),
        pltpu.VMEM((2, FOLD, 512), F32),
        pltpu.VMEM((2, TILE, TILE), F32),
        pltpu.VMEM((14, BAND, TILE), F32),
    ]
    scratch += [pltpu.VMEM(c.shape, BF16) for c in consts]
    for n in (3, 6, 6, 6, 15, 15, 6, 6, 6, 6, 7, 7, 8, 7, 7, 14, 14):
        scratch.append(dma((n,)))
    stats = pl.pallas_call(
        kernel,
        out_shape=out,
        in_specs=[hbm] * 9,
        out_specs=vmem,
        scratch_shapes=scratch,
        name="match",
        compiler_params=pltpu.CompilerParams(
            collective_id=0, has_side_effects=True, vmem_limit_bytes=60 * 1024 * 1024
        ),
    )(micrograph, projections, orientations, *[jnp.asarray(c) for c in consts])
    return stats[0], stats[1] / 16.0, stats[2] / 16.0


def solution(mesh):
    in_specs = (P("oy", "ox"), P(("ox", "ori"), None, None), P("ori"))
    out_specs = (P(("oy", "ori"), "ox"), P(("oy", "ori"), "ox"), P(("oy", "ori"), "ox"))
    return jax.shard_map(body, mesh=mesh, in_specs=in_specs, out_specs=out_specs, check_vma=False)
```

time: 58.6 us -> 45 us (0.77)
  local copies, waits for them, and re-layouts: 11.2 us -> 0 us
  Pallas kernels: 46 us -> 42.8 us
  other arithmetic: 0 us -> 1.43 us
    unnamed x21 -> x0, local copies, waits for them, and re-layouts: 11.2 us -> none
    pallas_call x1, Pallas kernels: 46 us -> 42.8 us  [body(): pl.pallas_call(kernel, out_shape=out, in_specs=[hbm] * 9, out_specs=vmem,...]
    div x0 -> x1, other arithmetic: none -> 1.43 us  [body(): return (stats[0], stats[1] / 16.0, stats[2] / 16.0)]
where the time goes in v2:
time: 45 us; the launch traced here: 44.8 us
  Pallas kernels  42.8 us (95%)
  other arithmetic  1.43 us (3%)
  between operations  0.64 us (1%)
    pallas_call x1, Pallas kernels, body(): pl.pallas_call(kernel, out_shape=out, in_specs=[hbm] * 9, out_specs=vmem,...  42.8 us
    div x1, other arithmetic, body(): return (stats[0], stats[1] / 16.0, stats[2] / 16.0)  1.43 us

profile of v2, /device:TPU:1, one launch (start us, length us, event | category | flops | bytes accessed | tf_op | source)
XLA Modules:
  0.0 44.8 jit_solution(3719557283369204140)
XLA Ops:
  0.6 42.8 %match.1 = f32[3,32,256]{2,1,0:T(8,128)} custom-call(f32[256,256]{1,0:T(8,128)} %x_ref.1, bf16[1,192,192]{2,1,0:T(8,128)(2,1)} %t_ref.1, s32[2]{0:T(128)} %o_ref.1, bf16[1536,512]{1,0:T(8,128)(2,1)} %constant.16.clone.ix_h, bf16[2,224,672]{2,1,0:T(8,128)(2,1)} %constant.17.clone.iy_h, bf16[512,512]{1,0:T(8,128)(2,1)} %constant.18.clone.bx_h, ...), custom_call_target="tpu_custom_call" | custom-call | tf_op jit(solution)/shard_map/match/pallas_call | solution.py:473
  43.4 1.4 %multiply_bitcast_fusion = (f32[32,256]{1,0:T(8,128)}, f32[32,256]{1,0:T(8,128)}, f32[32,256]{1,0:T(8,128)}) fusion(f32[3,32,256]{2,1,0:T(8,128)} %match.1), kind=kLoop, calls=%fused_computation | loop fusion | flops 16384 | bytes 196608 | tf_op jit(solution)/shard_map/div | solution.py:484

commit v3 on v2

--- a/solution.py
+++ b/solution.py
@@ -285,51 +285,24 @@
         def _(n=n):
             corners(n).start()
 
-    for copy_of in (straight, corners):
-        for n in range(2):
-
-            @pl.when(sides[n][1])
-            def _(n=n, copy_of=copy_of):
-                copy_of(n).wait_send()
-
-            @pl.when(sides[n][2])
-            def _(n=n, copy_of=copy_of):
-                copy_of(n).wait_recv()
-
-    for r_at, r_size, r_ok in ((0, 256, None), (256, HALF, z < 7), (352, HALF, z > 0)):
-        for c_at, c_size, c_ok in ((0, 256, None), (256, 128, a < 7), (384, 128, a > 0)):
-            if r_at == 0 and c_at == 0:
-                values = pixels_in[...] - tile_mean
-            else:
-                values = ext[r_at : r_at + r_size, c_at : c_at + c_size] - tile_mean
-            for ok in (r_ok, c_ok):
-                if ok is not None:
-                    values = jnp.where(ok, values, 0.0)
-            high, low = split(values)
-            ext_hi[r_at : r_at + r_size, c_at : c_at + c_size] = high
-            ext_lo[r_at : r_at + r_size, c_at : c_at + c_size] = low
-
-    for load in loads:
-        load.wait()
-
-    for tau in range(2):
-        at = slice(tau * 256, tau * 256 + 256)
-        whole = jnp.concatenate([ext_hi[...], ext_lo[...], ext_hi[...]], axis=1)
-        lines = mul(whole, ix[:, at])
-        upper, lower = lines[:FOLD], lines[FOLD:]
-        even = mul(iy[0], left_of(upper + lower))
-        odd = mul(iy[1], left_of(upper - lower))
-        quarter = FOLD // 2
-        image[0, :, at], image[1, :, at] = both_ways(
-            jnp.concatenate([even[:quarter], odd[:quarter], even[quarter:], odd[quarter:]], axis=0)
-        )
-
     for d in range(1, 8):
 
         @pl.when(z + d < 8)
         def _(d=d):
             heard(d)
             tell(d, up_s).start()
+
+    for d in range(1, 8):
+
+        @pl.when(z - d >= 0)
+        def _(d=d):
+            heard(-d)
+
+    mid, dev = merge([stats_a.at[k] for k in range(8)], count)
+    stat_b[...] = jnp.where(row == 0, mid, dev)
+    stat_copies = [
+        send(stat_b, stats_b.at[k], sb_s.at[k], sb_r.at[k], peer) for k, peer in enumerate(ox_peers)
+    ]
 
     box_copies = []
     for slot in range(2):
@@ -345,17 +318,44 @@
                 send(piece.at[slot], boxes.at[slot, core, mid_rows], box_s.at[n], box_r.at[n], peer)
             )
 
-    for d in range(1, 8):
-
-        @pl.when(z - d >= 0)
-        def _(d=d):
-            heard(-d)
-
-    mid, dev = merge([stats_a.at[k] for k in range(8)], count)
-    stat_b[...] = jnp.where(row == 0, mid, dev)
-    stat_copies = [
-        send(stat_b, stats_b.at[k], sb_s.at[k], sb_r.at[k], peer) for k, peer in enumerate(ox_peers)
-    ]
+    for copy_of in (straight, corners):
+        for n in range(2):
+
+            @pl.when(sides[n][1])
+            def _(n=n, copy_of=copy_of):
+                copy_of(n).wait_send()
+
+            @pl.when(sides[n][2])
+            def _(n=n, copy_of=copy_of):
+                copy_of(n).wait_recv()
+
+    for r_at, r_size, r_ok in ((0, 256, None), (256, HALF, z < 7), (352, HALF, z > 0)):
+        for c_at, c_size, c_ok in ((0, 256, None), (256, 128, a < 7), (384, 128, a > 0)):
+            if r_at == 0 and c_at == 0:
+                values = pixels_in[...] - tile_mean
+            else:
+                values = ext[r_at : r_at + r_size, c_at : c_at + c_size] - tile_mean
+            for ok in (r_ok, c_ok):
+                if ok is not None:
+                    values = jnp.where(ok, values, 0.0)
+            high, low = split(values)
+            ext_hi[r_at : r_at + r_size, c_at : c_at + c_size] = high
+            ext_lo[r_at : r_at + r_size, c_at : c_at + c_size] = low
+
+    for load in loads:
+        load.wait()
+
+    for tau in range(2):
+        at = slice(tau * 256, tau * 256 + 256)
+        whole = jnp.concatenate([ext_hi[...], ext_lo[...], ext_hi[...]], axis=1)
+        lines = mul(whole, ix[:, at])
+        upper, lower = lines[:FOLD], lines[FOLD:]
+        even = mul(iy[0], left_of(upper + lower))
+        odd = mul(iy[1], left_of(upper - lower))
+        quarter = FOLD // 2
+        image[0, :, at], image[1, :, at] = both_ways(
+            jnp.concatenate([even[:quarter], odd[:quarter], even[quarter:], odd[quarter:]], axis=0)
+        )
 
     y_at = lax.broadcasted_iota(jnp.int32, (TILE, BOX), 0)
     u_at = lax.broadcasted_iota(jnp.int32, (TILE, BOX), 1)

time: 45 us -> 42.4 us (0.942)
  Pallas kernels: 42.8 us -> 40.1 us
    pallas_call x1, Pallas kernels: 42.8 us -> 40.1 us  [body(): pl.pallas_call(kernel, out_shape=out, in_specs=[hbm] * 9, out_specs=vmem,...]
where the time goes in v3:
time: 42.4 us; the launch traced here: 42.2 us
  Pallas kernels  40.1 us (95%)
  other arithmetic  1.43 us (3%)
  between operations  0.64 us (2%)
    pallas_call x1, Pallas kernels, body(): pl.pallas_call(kernel, out_shape=out, in_specs=[hbm] * 9, out_specs=vmem,...  40.1 us
    div x1, other arithmetic, body(): return (stats[0], stats[1] / 16.0, stats[2] / 16.0)  1.43 us

profile of v3, /device:TPU:1, one launch (start us, length us, event | category | flops | bytes accessed | tf_op | source)
XLA Modules:
  0.0 42.2 jit_solution(6101449710117195958)
XLA Ops:
  0.6 40.1 %match.1 = f32[3,32,256]{2,1,0:T(8,128)} custom-call(f32[256,256]{1,0:T(8,128)} %x_ref.1, bf16[1,192,192]{2,1,0:T(8,128)(2,1)} %t_ref.1, s32[2]{0:T(128)} %o_ref.1, bf16[1536,512]{1,0:T(8,128)(2,1)} %constant.16.clone.ix_h, bf16[2,224,672]{2,1,0:T(8,128)(2,1)} %constant.17.clone.iy_h, bf16[512,512]{1,0:T(8,128)(2,1)} %constant.18.clone.bx_h, ...), custom_call_target="tpu_custom_call" | custom-call | tf_op jit(solution)/shard_map/match/pallas_call | solution.py:473
  40.8 1.4 %multiply_bitcast_fusion = (f32[32,256]{1,0:T(8,128)}, f32[32,256]{1,0:T(8,128)}, f32[32,256]{1,0:T(8,128)}) fusion(f32[3,32,256]{2,1,0:T(8,128)} %match.1), kind=kLoop, calls=%fused_computation | loop fusion | flops 16384 | bytes 196608 | tf_op jit(solution)/shard_map/div | solution.py:484

commit v4 on v3

--- a/solution.py
+++ b/solution.py
@@ -19,9 +19,11 @@
 HALF = 96
 LEN = 448
 FOLD = LEN // 2
-PART = 96
+ROWS = 288
+PART = 80
 BAND = 32
 FREQS = LEN // 2 + 1
+FAR_FIRST = (2, 6, 3, 5, 1, 7, 4)
 
 
 def trig(rows, cols):
@@ -133,7 +135,7 @@
     ori_peers = [{"ori": turn(j, d)} for d in range(1, 8)]
     pair_peers = [{"ox": partner, "ori": turn(j, d)} for d in range(8)]
     ox_peers = [{"ox": turn(a, d)} for d in range(1, 8)]
-    hi_peers = [{"ox": turn(a, 2 * d)} for d in range(1, 4)]
+    hi_peers = [{"ox": turn(a, 2 * d)} for d in (2, 1, 3)]
     box_peers = [{"ox": partner}, {"oy": beside}, {"oy": beside, "ox": partner}]
 
     barrier = pltpu.get_barrier_semaphore()
@@ -141,6 +143,8 @@
     def greet(peer):
         pl.semaphore_signal(barrier, inc=1, device_id=peer, device_id_type=MESH)
 
+    for peer in ox_peers + pair_peers[1:] + ori_peers + box_peers[2:]:
+        greet(peer)
     sides = ((1, z < 7, z > 0), (-1, z > 0, z < 7))
     for dz, there, _ in sides:
 
@@ -148,8 +152,6 @@
         def _(dz=dz):
             greet({"oy": z + dz})
 
-    for peer in ox_peers + pair_peers[1:] + ori_peers + box_peers[2:]:
-        greet(peer)
     for d in range(2, 8):
 
         @pl.when(z + d < 8)
@@ -178,9 +180,9 @@
     for load in own_loads:
         load.wait()
 
-    own[0] = box_in[0, :, 0:128]
-    own[1] = jnp.zeros((BOX, 128), BF16)
-    own[1, :, 0 : BOX - 128] = box_in[0, :, 128:BOX]
+    own[0:BOX] = box_in[0, :, 0:128]
+    tail = box_in[0, :, 128:BOX].astype(F32)
+    own[BOX:ROWS] = jnp.concatenate([tail[: BOX // 2], tail[BOX // 2 :]], axis=1).astype(BF16)
 
     pixels = pixels_in[...]
     count = float(TILE * TILE)
@@ -203,14 +205,20 @@
         copy.start()
         return copy
 
-    mid_rows = pl.ds(pl.multiple_of(half * PART, 16), PART)
+    def part_of(core):
+        return pl.ds(pl.multiple_of(half * (ROWS // 2) + core * 64, 16), PART)
+
     bank_copies = [
-        send(
-            own.at[core if k < 7 else 1 - core, mid_rows],
+        copier(
+            own.at[part_of(core if k < 7 else 1 - core)],
             bank.at[k], bank_s.at[k], bank_r.at[k], peer,
         )
         for k, peer in enumerate(ori_peers + pair_peers)
     ]
+    for d in FAR_FIRST:
+        bank_copies[7 + d].start()
+        bank_copies[d - 1].start()
+    bank_copies[7].start()
 
     def tell(d, s):
         return copier(stat_a, stats_a.at[z], s.at[abs(d) - 1], sa_r.at[z], {"oy": z + d})
@@ -254,7 +262,7 @@
 
     totals = []
     for slot in range(2):
-        local = own[core, mid_rows, :].astype(F32)
+        local = own[part_of(core), :].astype(F32)
         totals.append(jnp.where(a * 8 + j == wanted[slot], 1.0, 0.0) * local)
     for k, copy in enumerate(bank_copies):
         copy.wait()
@@ -311,11 +319,10 @@
             some_copies[slot * 3 + k].wait()
             total += some[slot * 3 + k].astype(F32)
         piece[slot] = total.astype(BF16)
-        boxes[slot, core, mid_rows, :] = piece[slot]
         for k, peer in enumerate(box_peers):
             n = slot * 3 + k
             box_copies.append(
-                send(piece.at[slot], boxes.at[slot, core, mid_rows], box_s.at[n], box_r.at[n], peer)
+                send(piece.at[slot], boxes.at[n], box_s.at[n], box_r.at[n], peer)
             )
 
     for copy_of in (straight, corners):
@@ -364,13 +371,32 @@
     v_at = lax.broadcasted_iota(jnp.int32, (TILE, TILE), 0)
     x_at = lax.broadcasted_iota(jnp.int32, (TILE, TILE), 1)
     line = a * TILE + x_at + v_at - HALF
-    col_in = jnp.where((line >= 0) & (line < 8 * TILE), 1.0, 0.0).astype(BF16)
+    col_in = jnp.where((line >= 0) & (line < 8 * TILE) & (v_at < BOX), 1.0, 0.0).astype(BF16)
 
     out_copies = []
     for slot in range(2):
         for k in range(3):
             box_copies[slot * 3 + k].wait()
-        box = jnp.concatenate([boxes[slot, 0], boxes[slot, 1]], axis=1)
+        here, there = (
+            [first.astype(F32), second.astype(F32)]
+            for first, second in (
+                (piece[slot], boxes[slot * 3]),
+                (boxes[slot * 3 + 1], boxes[slot * 3 + 2]),
+            )
+        )
+        here, there = (
+            jnp.concatenate(
+                [jnp.where(core == 0, p, q), jnp.where(core == 0, q, p)[2 * PART - ROWS // 2 :]],
+                axis=0,
+            )
+            for p, q in (here, there)
+        )
+        flat = jnp.concatenate(
+            [jnp.where(half == 0, here, there), jnp.where(half == 0, there, here)], axis=0
+        )
+        tail = flat[BOX:]
+        tail = jnp.concatenate([tail, pltpu.roll(tail, 64, 1)], axis=0)
+        box = jnp.concatenate([flat[:BOX].astype(BF16), tail.astype(BF16)], axis=1)
 
         twice = jnp.concatenate([box, box], axis=1)
         parts = []
@@ -405,7 +431,7 @@
             rest = mid[:, 0:1] - tile_mean
         corr[slot] = parts[0] + parts[1] - rest * cover
 
-        for d in range(1, 8):
+        for d in FAR_FIRST:
             to = turn(j, d)
             k = slot * 7 + d - 1
             out_copies.append(
@@ -420,8 +446,9 @@
     best = jnp.maximum(one, two)
     summed = one + two
     squared = one * one + two * two
-    for k, copy in enumerate(out_copies):
+    for copy in out_copies:
         copy.wait()
+    for k in range(14):
         value = got[k]
         best = jnp.maximum(best, value)
         summed += value
@@ -453,12 +480,12 @@
         pltpu.VMEM((LEN, 512), F32),
         pltpu.VMEM((LEN, 512), BF16),
         pltpu.VMEM((LEN, 512), BF16),
-        pltpu.VMEM((2, BOX, 128), BF16),
+        pltpu.VMEM((ROWS, 128), BF16),
         pltpu.VMEM((15, PART, 128), BF16),
         pltpu.VMEM((2, PART, 128), BF16),
         pltpu.VMEM((6, PART, 128), BF16),
         pltpu.VMEM((2, PART, 128), BF16),
-        pltpu.VMEM((2, 2, BOX, 128), BF16),
+        pltpu.VMEM((6, PART, 128), BF16),
         pltpu.VMEM((8, 128), F32),
         pltpu.VMEM((8, 8, 128), F32),
         pltpu.VMEM((8, 128), F32),

time: 42.4 us -> 40.1 us (0.946)
  Pallas kernels: 40.1 us -> 37.9 us
    pallas_call x1, Pallas kernels: 40.1 us -> 37.9 us  [body(): pl.pallas_call(kernel, out_shape=out, in_specs=[hbm] * 9, out_specs=vmem,...]
where the time goes in v4:
time: 40.1 us; the launch traced here: 39.9 us
  Pallas kernels  37.9 us (95%)
  other arithmetic  1.43 us (4%)
  between operations  0.64 us (2%)
    pallas_call x1, Pallas kernels, body(): pl.pallas_call(kernel, out_shape=out, in_specs=[hbm] * 9, out_specs=vmem,...  37.9 us
    div x1, other arithmetic, body(): return (stats[0], stats[1] / 16.0, stats[2] / 16.0)  1.43 us

profile of v4, /device:TPU:1, one launch (start us, length us, event | category | flops | bytes accessed | tf_op | source)
XLA Modules:
  0.0 39.9 jit_solution(13999310120218001240)
XLA Ops:
  0.6 37.9 %match.1 = f32[3,32,256]{2,1,0:T(8,128)} custom-call(f32[256,256]{1,0:T(8,128)} %x_ref.1, bf16[1,192,192]{2,1,0:T(8,128)(2,1)} %t_ref.1, s32[2]{0:T(128)} %o_ref.1, bf16[1536,512]{1,0:T(8,128)(2,1)} %constant.16.clone.ix_h, bf16[2,224,672]{2,1,0:T(8,128)(2,1)} %constant.17.clone.iy_h, bf16[512,512]{1,0:T(8,128)(2,1)} %constant.18.clone.bx_h, ...), custom_call_target="tpu_custom_call" | custom-call | tf_op jit(solution)/shard_map/match/pallas_call | solution.py:500
  38.5 1.4 %multiply_bitcast_fusion = (f32[32,256]{1,0:T(8,128)}, f32[32,256]{1,0:T(8,128)}, f32[32,256]{1,0:T(8,128)}) fusion(f32[3,32,256]{2,1,0:T(8,128)} %match.1), kind=kLoop, calls=%fused_computation | loop fusion | flops 16384 | bytes 196608 | tf_op jit(solution)/shard_map/div | solution.py:511

commit v5 on v4

--- a/solution.py
+++ b/solution.py
@@ -80,7 +80,7 @@
     cosine, sine = trig(freq, pixel)
     share = np.where((freq == 0) | (freq == FREQS - 1), 1.0, 2.0) * live / (LEN * LEN)
     back_x = by_tile(cosine * share[:, None], -sine * share[:, None], 0)
-    back_x = stacked(back_x.reshape(2, 256, TILE), 1, "hhl")
+    back_x = stacked(back_x, 0, "hhl")
     return [image_x, image_y, box_x, box_y, back_y, back_x]
 
 
@@ -138,6 +138,13 @@
     hi_peers = [{"ox": turn(a, 2 * d)} for d in (2, 1, 3)]
     box_peers = [{"ox": partner}, {"oy": beside}, {"oy": beside, "ox": partner}]
 
+    own_loads = [
+        pltpu.make_async_copy(src, dst, own_sem.at[k])
+        for k, (src, dst) in enumerate(((x_ref, pixels_in), (t_ref, box_in), (o_ref, wanted)))
+    ]
+    for load in own_loads:
+        load.start()
+
     barrier = pltpu.get_barrier_semaphore()
 
     def greet(peer):
@@ -165,24 +172,67 @@
         + jnp.where(z > 1, z - 1, 0)
     )
 
-    own_loads = [
-        pltpu.make_async_copy(src, dst, own_sem.at[k])
-        for k, (src, dst) in enumerate(((x_ref, pixels_in), (t_ref, box_in), (o_ref, wanted)))
-    ]
-    loads = [
-        pltpu.make_async_copy(src, dst, table_sem.at[k])
-        for k, (src, dst) in enumerate(
-            ((ix_h, ix), (iy_h, iy), (bx_h, bx), (by_h, by), (ky_h, ky), (kx_h, kx))
-        )
-    ]
-    for load in own_loads + loads:
-        load.start()
     for load in own_loads:
         load.wait()
 
     own[0:BOX] = box_in[0, :, 0:128]
     tail = box_in[0, :, 128:BOX].astype(F32)
     own[BOX:ROWS] = jnp.concatenate([tail[: BOX // 2], tail[BOX // 2 :]], axis=1).astype(BF16)
+
+    pl.semaphore_wait(barrier, greetings)
+
+    def copier(src, dst, s, r, peer):
+        return pltpu.make_async_remote_copy(
+            src_ref=src, dst_ref=dst, send_sem=s, recv_sem=r, device_id=peer, device_id_type=MESH
+        )
+
+    def send(*what):
+        copy = copier(*what)
+        copy.start()
+        return copy
+
+    def part_of(core):
+        return pl.ds(pl.multiple_of(half * (ROWS // 2) + core * 64, 16), PART)
+
+    bank_copies = [
+        copier(
+            own.at[part_of(core if k < 7 else 1 - core)],
+            bank.at[k], bank_s.at[k], bank_r.at[k], peer,
+        )
+        for k, peer in enumerate(ori_peers + pair_peers)
+    ]
+    for d in FAR_FIRST:
+        bank_copies[7 + d].start()
+        bank_copies[d - 1].start()
+    bank_copies[7].start()
+
+    row_kind = {-1: (0, 256), 1: (TILE - HALF, 352)}
+    across = [
+        send(
+            pixels_in.at[:, pl.ds(c_from, 128)], ext.at[pl.ds(0, TILE), pl.ds(c_to, 128)],
+            halo_s.at[k], halo_r.at[k], {"ox": turn(a, da)},
+        )
+        for k, (da, c_from, c_to) in enumerate(((1, 128, 384), (7, 0, 256)))
+    ]
+
+    def along(k, dz, source, lanes):
+        r_from, r_to = row_kind[dz]
+        return copier(
+            source.at[pl.ds(r_from, HALF), lanes], ext.at[pl.ds(r_to, HALF), lanes],
+            halo_s.at[k], halo_r.at[k], {"oy": z + dz},
+        )
+
+    def straight(n):
+        return along(2 + n, sides[n][0], pixels_in, pl.ds(0, 256))
+
+    def corners(n):
+        return along(4 + n, sides[n][0], ext, pl.ds(256, 256))
+
+    for n in range(2):
+
+        @pl.when(sides[n][1])
+        def _(n=n):
+            straight(n).start()
 
     pixels = pixels_in[...]
     count = float(TILE * TILE)
@@ -193,33 +243,6 @@
     stat_a[...] = jnp.where(row == 0, tile_mean, tile_dev)
     stats_a[z] = stat_a[...]
 
-    pl.semaphore_wait(barrier, greetings)
-
-    def copier(src, dst, s, r, peer):
-        return pltpu.make_async_remote_copy(
-            src_ref=src, dst_ref=dst, send_sem=s, recv_sem=r, device_id=peer, device_id_type=MESH
-        )
-
-    def send(*what):
-        copy = copier(*what)
-        copy.start()
-        return copy
-
-    def part_of(core):
-        return pl.ds(pl.multiple_of(half * (ROWS // 2) + core * 64, 16), PART)
-
-    bank_copies = [
-        copier(
-            own.at[part_of(core if k < 7 else 1 - core)],
-            bank.at[k], bank_s.at[k], bank_r.at[k], peer,
-        )
-        for k, peer in enumerate(ori_peers + pair_peers)
-    ]
-    for d in FAR_FIRST:
-        bank_copies[7 + d].start()
-        bank_copies[d - 1].start()
-    bank_copies[7].start()
-
     def tell(d, s):
         return copier(stat_a, stats_a.at[z], s.at[abs(d) - 1], sa_r.at[z], {"oy": z + d})
 
@@ -232,33 +255,14 @@
         def _(d=d):
             tell(-d, down_s).start()
 
-    row_kind = {-1: (0, 256), 1: (TILE - HALF, 352)}
-    across = [
-        send(
-            pixels_in.at[:, pl.ds(c_from, 128)], ext.at[pl.ds(0, TILE), pl.ds(c_to, 128)],
-            halo_s.at[k], halo_r.at[k], {"ox": turn(a, da)},
-        )
-        for k, (da, c_from, c_to) in enumerate(((1, 128, 384), (7, 0, 256)))
+    loads = [
+        pltpu.make_async_copy(src, dst, table_sem.at[k])
+        for k, (src, dst) in enumerate(
+            ((ix_h, ix), (iy_h, iy), (bx_h, bx), (by_h, by), (ky_h, ky), (kx_h, kx))
+        )
     ]
-
-    def along(k, dz, source, lanes):
-        r_from, r_to = row_kind[dz]
-        return copier(
-            source.at[pl.ds(r_from, HALF), lanes], ext.at[pl.ds(r_to, HALF), lanes],
-            halo_s.at[k], halo_r.at[k], {"oy": z + dz},
-        )
-
-    def straight(n):
-        return along(2 + n, sides[n][0], pixels_in, pl.ds(0, 256))
-
-    def corners(n):
-        return along(4 + n, sides[n][0], ext, pl.ds(256, 256))
-
-    for n in range(2):
-
-        @pl.when(sides[n][1])
-        def _(n=n):
-            straight(n).start()
+    for load in loads:
+        load.start()
 
     totals = []
     for slot in range(2):
@@ -322,8 +326,10 @@
         for k, peer in enumerate(box_peers):
             n = slot * 3 + k
             box_copies.append(
-                send(piece.at[slot], boxes.at[n], box_s.at[n], box_r.at[n], peer)
+                copier(piece.at[slot], boxes.at[n], box_s.at[n], box_r.at[n], peer)
             )
+        for k in (2, 1, 0):
+            box_copies[slot * 3 + k].start()
 
     for copy_of in (straight, corners):
         for n in range(2):
@@ -352,17 +358,16 @@
     for load in loads:
         load.wait()
 
+    whole = jnp.concatenate([ext_hi[...], ext_lo[...], ext_hi[...]], axis=1)
+    lines = mul(whole, ix[...])
+    upper, lower = lines[:FOLD], lines[FOLD:]
+    even = mul(iy[0], left_of(upper + lower))
+    odd = mul(iy[1], left_of(upper - lower))
+    quarter = FOLD // 2
+    both = jnp.concatenate([even[:quarter], odd[:quarter], even[quarter:], odd[quarter:]], axis=0)
     for tau in range(2):
         at = slice(tau * 256, tau * 256 + 256)
-        whole = jnp.concatenate([ext_hi[...], ext_lo[...], ext_hi[...]], axis=1)
-        lines = mul(whole, ix[:, at])
-        upper, lower = lines[:FOLD], lines[FOLD:]
-        even = mul(iy[0], left_of(upper + lower))
-        odd = mul(iy[1], left_of(upper - lower))
-        quarter = FOLD // 2
-        image[0, :, at], image[1, :, at] = both_ways(
-            jnp.concatenate([even[:quarter], odd[:quarter], even[quarter:], odd[quarter:]], axis=0)
-        )
+        image[0, :, at], image[1, :, at] = both_ways(both[:, at])
 
     y_at = lax.broadcasted_iota(jnp.int32, (TILE, BOX), 0)
     u_at = lax.broadcasted_iota(jnp.int32, (TILE, BOX), 1)
@@ -399,13 +404,14 @@
         box = jnp.concatenate([flat[:BOX].astype(BF16), tail.astype(BF16)], axis=1)
 
         twice = jnp.concatenate([box, box], axis=1)
-        parts = []
+        wave = mul(by[...], left_of(mul(twice, bx[...])))
+        first = lax.broadcasted_iota(jnp.int32, (FOLD, 128), 0) == 0
+        joints = []
         for tau in range(2):
             at = slice(tau * 256, tau * 256 + 256)
-            t_plus, t_minus = both_ways(mul(by[...], left_of(mul(twice, bx[:, at]))))
+            t_plus, t_minus = both_ways(wave[:, at])
             p_re, p_im = conj_product(image[0, :, at], t_plus)
             m_re, m_im = conj_product(image[1, :, at], t_minus)
-            first = lax.broadcasted_iota(jnp.int32, (FOLD, 128), 0) == 0
             joint = jnp.concatenate(
                 [
                     jnp.concatenate(
@@ -419,7 +425,9 @@
                 ],
                 axis=0,
             )
-            parts.append(mul(left_of(mul(ky[...], left_of(joint)), 1), kx[tau]))
+            joints.append(joint)
+        lines = mul(ky[...], left_of(jnp.concatenate(joints, axis=1)))
+        found = mul(left_of(lines, 1), kx[...])
         high, low = split(mul(row_in, box))
         cover = mul(high, col_in) + mul(low, col_in)
 
@@ -429,7 +437,7 @@
             mid, dev = merge([stat_b] + [stats_b.at[k] for k in range(7)], count * 8)
             scale = 1.0 / jnp.sqrt(dev[:, 0:1] / (count * 64) + 1e-06)
             rest = mid[:, 0:1] - tile_mean
-        corr[slot] = parts[0] + parts[1] - rest * cover
+        corr[slot] = found - rest * cover
 
         for d in FAR_FIRST:
             to = turn(j, d)

time: 40.1 us -> 39 us (0.973)
  Pallas kernels: 37.9 us -> 36.5 us
    pallas_call x1, Pallas kernels: 37.9 us -> 36.5 us  [body(): pl.pallas_call(kernel, out_shape=out, in_specs=[hbm] * 9, out_specs=vmem,...]
where the time goes in v5:
time: 39 us; the launch traced here: 38.6 us
  Pallas kernels  36.5 us (94%)
  other arithmetic  1.43 us (4%)
  between operations  0.64 us (2%)
    pallas_call x1, Pallas kernels, body(): pl.pallas_call(kernel, out_shape=out, in_specs=[hbm] * 9, out_specs=vmem,...  36.5 us
    div x1, other arithmetic, body(): return (stats[0], stats[1] / 16.0, stats[2] / 16.0)  1.43 us

profile of v5, /device:TPU:1, one launch (start us, length us, event | category | flops | bytes accessed | tf_op | source)
XLA Modules:
  0.0 38.6 jit_solution(15475864019007335550)
XLA Ops:
  0.6 36.5 %match.1 = f32[3,32,256]{2,1,0:T(8,128)} custom-call(f32[256,256]{1,0:T(8,128)} %x_ref.1, bf16[1,192,192]{2,1,0:T(8,128)(2,1)} %t_ref.1, s32[2]{0:T(128)} %o_ref.1, bf16[1536,512]{1,0:T(8,128)(2,1)} %constant.16.clone.ix_h, bf16[2,224,672]{2,1,0:T(8,128)(2,1)} %constant.17.clone.iy_h, bf16[512,512]{1,0:T(8,128)(2,1)} %constant.18.clone.bx_h, ...), custom_call_target="tpu_custom_call" | custom-call | tf_op jit(solution)/shard_map/match/pallas_call | solution.py:508
  37.2 1.4 %multiply_bitcast_fusion = (f32[32,256]{1,0:T(8,128)}, f32[32,256]{1,0:T(8,128)}, f32[32,256]{1,0:T(8,128)}) fusion(f32[3,32,256]{2,1,0:T(8,128)} %match.1), kind=kLoop, calls=%fused_computation | loop fusion | flops 16384 | bytes 196608 | tf_op jit(solution)/shard_map/div | solution.py:519

commit v6 on v5

--- a/solution.py
+++ b/solution.py
@@ -454,10 +454,9 @@
     best = jnp.maximum(one, two)
     summed = one + two
     squared = one * one + two * two
-    for copy in out_copies:
+    for n, copy in enumerate(out_copies):
         copy.wait()
-    for k in range(14):
-        value = got[k]
+        value = got[n // 7 * 7 + FAR_FIRST[n % 7] - 1]
         best = jnp.maximum(best, value)
         summed += value
         squared += value * value

time: 39 us -> 39 us (level)
  no operation moved by 1% of the time
where the time goes in v6:
time: 39 us; the launch traced here: 38.6 us
  Pallas kernels  36.5 us (94%)
  other arithmetic  1.43 us (4%)
  between operations  0.64 us (2%)
    pallas_call x1, Pallas kernels, body(): pl.pallas_call(kernel, out_shape=out, in_specs=[hbm] * 9, out_specs=vmem,...  36.5 us
    div x1, other arithmetic, body(): return (stats[0], stats[1] / 16.0, stats[2] / 16.0)  1.43 us

profile of v6, /device:TPU:1, one launch (start us, length us, event | category | flops | bytes accessed | tf_op | source)
XLA Modules:
  0.0 38.6 jit_solution(2351997554386177838)
XLA Ops:
  0.6 36.5 %match.1 = f32[3,32,256]{2,1,0:T(8,128)} custom-call(f32[256,256]{1,0:T(8,128)} %x_ref.1, bf16[1,192,192]{2,1,0:T(8,128)(2,1)} %t_ref.1, s32[2]{0:T(128)} %o_ref.1, bf16[1536,512]{1,0:T(8,128)(2,1)} %constant.16.clone.ix_h, bf16[2,224,672]{2,1,0:T(8,128)(2,1)} %constant.17.clone.iy_h, bf16[512,512]{1,0:T(8,128)(2,1)} %constant.18.clone.bx_h, ...), custom_call_target="tpu_custom_call" | custom-call | tf_op jit(solution)/shard_map/match/pallas_call | solution.py:507
  37.1 1.4 %multiply_bitcast_fusion = (f32[32,256]{1,0:T(8,128)}, f32[32,256]{1,0:T(8,128)}, f32[32,256]{1,0:T(8,128)}) fusion(f32[3,32,256]{2,1,0:T(8,128)} %match.1), kind=kLoop, calls=%fused_computation | loop fusion | flops 16384 | bytes 196608 | tf_op jit(solution)/shard_map/div | solution.py:518
